TPU v7x, 32 devices: a whole 2x2x4 slice. The times are simulated.
32 devices in a mesh: groups: 2 (over x), tensor: 16 (over z, y, core).
Axes of the slice: x: 2, y: 2, z: 4, core: 2. Of those that a mesh axis runs over, the one named last changes fastest.
Arguments:
- tokens: bfloat16 [1024, 8192], P(('groups', 'tensor')), parts along dimension 0, may hold values from -6 to 6
- attn_gain: float32 [8192], replicated, may hold values from 0.6 to 10, as said below
- w_query: bfloat16 [8192, 8192], P(None, 'tensor'), may hold values from -0.0625 to 0.0625
- w_key: bfloat16 [8192, 1024], P(None, 'tensor'), may hold values from -0.0625 to 0.0625
- w_value: bfloat16 [8192, 1024], P(None, 'tensor'), may hold values from -0.0625 to 0.0625
- w_output: bfloat16 [8192, 8192], P('tensor'), may hold values from -0.0625 to 0.0625
- doc_ids: int32 [1024], P('groups'), parts along dimension 0, may hold values from 0 to 3, never falling along the last dimension, each value on 1 to 256 neighbouring positions
Outputs:
- attention: bfloat16 [1024, 8192], P(('groups', 'tensor')), parts along dimension 0
- hidden: bfloat16 [1024, 8192], P(('groups', 'tensor')), parts along dimension 0
There are 2 independent parts, one for each index of `groups`. A program takes and returns all parts, laid end to end along the dimension named above; an argument that names none is the same for every part. Nothing has to cross between parts.
Inputs may be any that keep to these rules, and one draw needn't show every extreme that they name: `doc_ids`: document numbers never fall along the block, each document has 1 to 256 tokens and one has exactly that many. `attn_gain`: positive gains.
All inputs are finite; a program needn't handle non-finite values.
Results may differ from a plain program's by a relative error of at most 0.015.
The roundings to bfloat16 on the way count: a program that leaves them out, or rounds other values in their place, can miss the bound.
Values may be sent and summed in bfloat16 or wider, within the bound.
A program may use at most 128 MiB of HBM per device.

v0:
```python
import jax
import jax.numpy as jnp
from jax import lax
from jax.sharding import PartitionSpec as P

HEAD_DIM = 128


def swapped(value, axis, apart):
    mask = 2**apart
    pairs = [(source, source ^ mask) for source in range(lax.axis_size(axis))]
    return lax.ppermute(value, axis, pairs)


def rotary_angles(doc_ids, head_dim):
    count = doc_ids.shape[0]
    first = jnp.sum((doc_ids[None, :] < doc_ids[:, None]).astype(jnp.int32), axis=1)
    position = (jnp.arange(count, dtype=jnp.int32) - first).astype(jnp.float32)
    freq = jnp.float32(500000.0) ** (
        -(jnp.arange(head_dim // 2, dtype=jnp.float32) * 2.0 / head_dim)
    )
    angle = position[:, None] * freq[None, :]
    return (jnp.cos(angle)[:, None, :], jnp.sin(angle)[:, None, :])


def apply_rope(vectors, cosine, sine):
    half = vectors.shape[-1] // 2
    first_half = vectors[..., :half]
    second_half = vectors[..., half:]
    return jnp.concatenate(
        [first_half * cosine - second_half * sine, second_half * cosine + first_half * sine],
        axis=-1,
    )


def join_cols(mine, other, place, bit):
    upper = place // (1 << bit) % 2 == 1
    lower_part = jnp.where(upper, other, mine)
    upper_part = jnp.where(upper, mine, other)
    return jnp.concatenate([lower_part, upper_part], axis=-1)


def body(tokens, attn_gain, w_query, w_key, w_value, w_output, doc_ids):
    rows = tokens.astype(jnp.float32)
    normed_local = (
        rows * lax.rsqrt(jnp.mean(rows * rows, axis=-1, keepdims=True) + 1e-05) * attn_gain
    ).astype(jnp.bfloat16)
    normed = lax.all_gather(normed_local, "tensor", axis=0, tiled=True)
    count = normed.shape[0]
    head_dim = HEAD_DIM
    heads_here = w_query.shape[1] // head_dim
    cosine, sine = rotary_angles(doc_ids, head_dim)
    query_raw = jnp.dot(normed, w_query, preferred_element_type=jnp.float32).reshape(
        count, heads_here, head_dim
    )
    queries = apply_rope(query_raw, cosine, sine).astype(jnp.bfloat16)
    sharing = head_dim // w_key.shape[1]
    levels = sharing.bit_length() - 1
    place = lax.axis_index("tensor")
    stacked = jnp.stack([w_key, w_value])
    for bit in range(levels):
        partner = swapped(stacked, "tensor", bit)
        stacked = join_cols(stacked, partner, place, bit)
    kv_raw = jnp.einsum("td,sdc->stc", normed, stacked, preferred_element_type=jnp.float32).astype(
        jnp.bfloat16
    )
    keys = apply_rope(kv_raw[0].astype(jnp.float32)[:, None, :], cosine, sine)[:, 0, :].astype(
        jnp.bfloat16
    )
    values = kv_raw[1]
    index = jnp.arange(count, dtype=jnp.int32)
    block = min(512, count)
    scale = 1.0 / jnp.sqrt(jnp.float32(head_dim))
    pieces = []
    for begin in range(0, count, block):
        q_block = queries[begin : begin + block]
        scores = (
            jnp.einsum("qhd,kd->hqk", q_block, keys, preferred_element_type=jnp.float32) * scale
        )
        visible = (index[None, :] <= index[begin : begin + block, None]) & (
            doc_ids[None, :] == doc_ids[begin : begin + block, None]
        )
        scores = jnp.where(visible[None], scores, jnp.float32(-1e30))
        top = jnp.max(scores, axis=-1, keepdims=True)
        weights = jnp.exp(scores - top)
        probs = (weights / jnp.sum(weights, axis=-1, keepdims=True)).astype(jnp.bfloat16)
        result = jnp.einsum(
            "hqk,kd->qhd", probs, values, preferred_element_type=jnp.float32
        ).astype(jnp.bfloat16)
        pieces.append(result.reshape(block, heads_here * head_dim))
    attended = jnp.concatenate(pieces, axis=0)
    total = lax.psum_scatter(
        jnp.dot(attended, w_output, preferred_element_type=jnp.float32).astype(jnp.bfloat16),
        "tensor",
        scatter_dimension=0,
        tiled=True,
    ).astype(jnp.float32)
    return (total.astype(jnp.bfloat16), (rows + total).astype(jnp.bfloat16))


def solution(mesh):
    placed = (
        P(("groups", "tensor"), None),
        P(),
        P(None, "tensor"),
        P(None, "tensor"),
        P(None, "tensor"),
        P("tensor", None),
        P("groups"),
    )
    return jax.shard_map(
        body,
        mesh=mesh,
        in_specs=placed,
        out_specs=(P(("groups", "tensor"), None), P(("groups", "tensor"), None)),
        check_vma=False,
    )
```

profile of v0, /device:TPU:0, one launch (start us, length us, event | category | flops | bytes accessed | tf_op | source)
XLA Modules:
  0.0 231.2 jit_solution(4767195997888019148)
XLA Ops:
  7.2 1.4 fusion.22
  8.6 2.0 fusion.24
  10.7 3.1 %pad_maximum_fusion = bf16[2,8192,64]{1,2,0:T(8,128)(2,1)} fusion(bf16[1,8192,64]{1,2,0:T(8,128)(2,1)} %bitcast.46, bf16[1,8192,64]{1,2,0:T(8,128)(2,1)} %bitcast.48), kind=kLoop, calls=%fused_computation.11 | loop fusion | flops 1048576 | bytes 4194304 | tf_op jit(solution)/shard_map/stack | solution.py:60
  13.8 0.5 collective-permute-start
  14.3 0.2 convert_reduce_fusion
  14.5 0.2 fusion.26
  14.7 1.0 multiply_cosine_fusion
  15.7 2.7 %collective-permute-done = bf16[2,8192,64]{1,2,0:T(8,128)(2,1)} collective-permute-done((bf16[2,8192,64]{1,2,0:T(8,128)(2,1)}, bf16[2,8192,64]{1,2,0:T(8,128)(2,1)}, u32[]{:S(2)}, u32[]{:S(2)}) %collective-permute-start) | collective-permute-done | bytes 2097184 | tf_op jit(solution)/shard_map/ppermute | solution.py:12
  18.4 3.9 %broadcast_select_fusion.1 = (bf16[2,8192,64]{1,2,0:T(8,128)(2,1)}, bf16[2,8192,64]{1,2,0:T(8,128)(2,1)}) fusion(bf16[2,8192,64]{1,2,0:T(8,128)(2,1)} %collective-permute-done, pred[]{:T(512)S(6)} %eq.22, bf16[1,8192,64]{1,2,0:T(8,128)(2,1)S(1)} %bitcast.47, bf16[1,8192,64]{1,2,0:T(8,128)(2,1)S(1)} %bitcast.49), kind=kLoop, calls=%fused_computation.17 | loop fusion | flops 3145728 | bytes 8388609 | tf_op jit(solution)/shard_map/jit(_where)/select_n | solution.py:38
  22.3 66.1 %all-gather.2.cloned.1.call-done = bf16[512,8192]{1,0:T(8,128)(2,1)} async-done(((bf16[32,8192]{1,0:T(8,128)(2,1)}), bf16[512,8192]{1,0:T(8,128)(2,1)}) %all-gather.2.cloned.1.call-update) | async-done | bytes 8388624 | tf_op jit(solution)/shard_map/all_gather | solution.py:48
  88.5 7.0 %fusion.17 = bf16[2,512,128]{1,2,0:T(8,128)(2,1)S(1)} fusion(bf16[512,8192]{1,0:T(8,128)(2,1)} %all-gather.2.cloned.1.call-done, bf16[2,8192,64]{1,2,0:T(8,128)(2,1)} %get-tuple-element.3, bf16[2,8192,64]{1,2,0:T(8,128)(2,1)} %get-tuple-element.2), kind=kOutput, calls=%fused_computation.23 | convolution fusion | flops 2156003328 | bytes 12845056 | tf_op jit(solution)/shard_map/td,sdc->stc/dot_general | solution.py:64
  95.5 0.7 copy-done.3
  96.2 0.6 fusion.36
  96.7 9.5 %fusion.48 = f32[512,512]{0,1:T(8,128)S(1)} fusion(bf16[512,8192]{1,0:T(8,128)(2,1)} %all-gather.2.cloned.1.call-done, bf16[8192,512]{1,0:T(8,128)(2,1)} %param.9), kind=kOutput, calls=%fused_computation.64 | convolution fusion | flops 4294967296 | bytes 17825792 | tf_op jit(solution)/shard_map/dot_general | solution.py:53
  106.3 0.3 copy.16
  106.7 0.3 copy.17
  107.0 0.3 subtract_convert_fusion
  107.3 0.8 fusion.27
  108.1 2.1 fusion.47
  110.3 0.5 fusion.11
  110.7 1.7 slice-done.1
  112.5 6.9 %convolution_convert_fusion = bf16[512,8192]{1,0:T(8,128)(2,1)} fusion(bf16[512,512]{0,1:T(8,128)(2,1)S(1)} %bitcast.51, bf16[512,8192]{1,0:T(8,128)(2,1)S(1)} %bitcast.45), kind=kOutput, calls=%fused_computation.1 | convolution fusion | flops 4299161600 | bytes 17301504 | tf_op jit(solution)/shard_map/dot_general | solution.py:93
  119.4 103.0 %reduce-scatter.2.cloned.1.call-done = bf16[32,8192]{1,0:T(8,128)(2,1)} async-done(((bf16[512,8192]{1,0:T(8,128)(2,1)}), bf16[32,8192]{1,0:T(8,128)(2,1)}) %reduce-scatter.2.cloned.1.call-update) | async-done | bytes 524304 | tf_op jit(solution)/shard_map/reduce_scatter | solution.py:92
  222.4 2.0 fusion.25
  (24 shorter events, 0.3 us)
Async XLA Ops:
  7.2 11.2 %copy-start.2 = (bf16[8192,64]{0,1:T(8,128)(2,1)S(1)}, bf16[8192,64]{0,1:T(8,128)(2,1)}, u32[]{:S(2)}) copy-start(bf16[8192,64]{0,1:T(8,128)(2,1)} %param.10) | copy-start | bytes 3145732
  7.2 11.2 %copy-start.1 = (bf16[8192,64]{0,1:T(8,128)(2,1)S(1)}, bf16[8192,64]{0,1:T(8,128)(2,1)}, u32[]{:S(2)}) copy-start(bf16[8192,64]{0,1:T(8,128)(2,1)} %param.11) | copy-start | bytes 3145732
  7.2 7.1 %copy-start.5 = (s32[512]{0:T(512)S(1)}, s32[512]{0:T(512)}, u32[]{:S(2)}) copy-start(s32[512]{0:T(512)} %param.13) | copy-start | bytes 6148
  7.2 81.3 %all-gather.2.cloned.1.call-start = ((), (), s32[]{:S(2)}) async-start(), calls=%async_computation.1 | async-start | bytes 8912896 | tf_op jit(solution)/shard_map/all_gather | solution.py:48
  10.7 211.7 %reduce-scatter.2.cloned.1.call-start = ((), (), s32[]{:S(2)}) async-start(), calls=%async_computation.2 | async-start | bytes 8912896 | tf_op jit(solution)/shard_map/reduce_scatter | solution.py:92
  13.8 4.6 %collective-permute-start = (bf16[2,8192,64]{1,2,0:T(8,128)(2,1)}, bf16[2,8192,64]{1,2,0:T(8,128)(2,1)}, u32[]{:S(2)}, u32[]{:S(2)}) collective-permute-start(bf16[2,8192,64]{1,2,0:T(8,128)(2,1)} %pad_maximum_fusion), channel_id=1, source_target_pairs={{0,1},{1,0},{2,3},{3,2},{4,5},{5,4},{6,7},{7,6},{8,9},{9,8},{10,11... | collective-permute-start | bytes 6291464 | tf_op jit(solution)/shard_map/ppermute | solution.py:12
  95.5 0.7 copy-start.3
  108.1 2.2 copy-start.4
  108.1 2.6 %slice-start = ((s8[8388608]{0:T(1024)(128)(4,1)}), s8[4194304]{0:T(1024)(128)(4,1)S(1)}, s32[]{:S(2)}) async-start(s8[8388608]{0:T(1024)(128)(4,1)} %bitcast.44), calls=%async_computation.3 | async-start | bytes 8388608
  110.3 2.2 slice-start.1
  119.4 103.0 %copy-start = (bf16[32,8192]{1,0:T(8,128)(2,1)S(1)}, bf16[32,8192]{1,0:T(8,128)(2,1)}, u32[]{:S(2)}) copy-start(bf16[32,8192]{1,0:T(8,128)(2,1)} %param.7) | copy-start | bytes 1572868
Sparse Core Ops, SparseCore 0:
  10.8 77.5 all-gather.1
  119.5 102.8 reduce-scatter.1
where the time goes:
time: 232 us; the launch traced here: 231 us
  waiting for transfers between devices  172 us (74%)
  matrix products  24.6 us (11%)
  other arithmetic  16.7 us (7%)
  between operations  14.2 us (6%)
  local copies, waits for them, and re-layouts  3.21 us (1%)
    reduce_scatter x1, waiting for transfers between devices, body(): lax.psum_scatter(jnp.dot(attended, w_output, preferred_element_type=jnp.f...  103 us
    all_gather x1, waiting for transfers between devices, body(): normed = lax.all_gather(normed_local, 'tensor', axis=0, tiled=True)  66.1 us
    dot_general x1, matrix products, body(): jnp.dot(normed, w_query, preferred_element_type=jnp.float32)  9.46 us
    dot_general x1, matrix products, body(): jnp.einsum('td,sdc->stc', normed, stacked, preferred_element_type=jnp.flo...  7.02 us
    dot_general x1, matrix products, body(): jnp.dot(attended, w_output, preferred_element_type=jnp.float32)  6.92 us
  transfers between devices with their start and end apart: 3, of which 3 were waited for; matrix products, arithmetic and copies ran while one was open for 4% of the time, Pallas kernels for 0%

commit v1 on v0

v1 whole, which is shorter than its diff:
```python
import functools
import jax
import jax.numpy as jnp
from jax import lax
from jax.experimental import pallas as pl
from jax.experimental.pallas import tpu as pltpu
from jax.sharding import PartitionSpec as P

HEAD_DIM = 128
HALVES = 2
PARTS = 4
MESH = pl.DeviceIdType.MESH
F32 = jnp.float32
BF16 = jnp.bfloat16


def swapped(value, axis, apart):
    mask = 2**apart
    pairs = [(source, source ^ mask) for source in range(lax.axis_size(axis))]
    return lax.ppermute(value, axis, pairs)


def join_cols(mine, other, place, bit):
    upper = place // (1 << bit) % 2 == 1
    lower_part = jnp.where(upper, other, mine)
    upper_part = jnp.where(upper, mine, other)
    return jnp.concatenate([lower_part, upper_part], axis=-1)


def chip_of(n, pos):
    if n == 8:
        second = lax.div(pos, 4)
        level = pos + second * (7 - 2 * pos)
        return 2 * level + second
    return pos


def pos_of(n, chip):
    if n == 8:
        level, second = lax.div(chip, 2), lax.rem(chip, 2)
        return level + second * (7 - 2 * level)
    return chip


def kernel(
    n, heads, shared,
    tokens, gain, wq, wk, wv, wo, docs, freq,
    att_out, hid_out,
    normed, wq_v, raw, wkv_v, wo_v, q_v, k_v, v_v, att_v, att_in, cos_v, sin_v, doc_v, inbox,
    ring_s, ring_r, fwd_s, fwd_r, kv_s, kv_r, wo_s, wo_r, at_s, at_r, rs_s, rs_r, loc,
):
    rows, width = tokens.shape
    count = normed.shape[0]
    piece = rows // HALVES
    cols = width // PARTS
    place = lax.axis_index("tensor")
    core = lax.rem(place, 2)
    chip = lax.div(place, 2)
    pos = pos_of(n, chip)
    way = 1 - 2 * core
    other = {"tensor": 2 * chip + 1 - core}

    def at_pos(p):
        return lax.rem(p + 2 * n, n)

    nxt = {"tensor": 2 * chip_of(n, at_pos(pos + way)) + core}
    prv = {"tensor": 2 * chip_of(n, at_pos(pos - way)) + core}

    def block_row(p, c):
        return pl.multiple_of((2 * chip_of(n, at_pos(p)) + c) * rows, rows)

    def remote(src, dst, s_sem, r_sem, to):
        return pltpu.make_async_remote_copy(
            src_ref=src, dst_ref=dst, send_sem=s_sem, recv_sem=r_sem,
            device_id=to, device_id_type=MESH,
        )

    def piece_at(p, c, h):
        return normed.at[pl.ds(pl.multiple_of(block_row(p, c) + h * piece, piece), piece), :]

    def ring(s, h):
        ref = piece_at(pos - way * s, core, h)
        return remote(ref, ref, ring_s.at[s, h], ring_r.at[s, h], nxt)

    def ring_in(s, h):
        ref = piece_at(pos - way * (s + 1), core, h)
        return remote(ref, ref, ring_s.at[s, h], ring_r.at[s, h], nxt)

    def fwd(s, h):
        ref = piece_at(pos - way * s, core, h)
        return remote(ref, ref, fwd_s.at[s, h], fwd_r.at[s, h], other)

    def fwd_in(s, h):
        ref = piece_at(pos + way * s, 1 - core, h)
        return remote(ref, ref, fwd_s.at[s, h], fwd_r.at[s, h], other)

    wo_piece = wo.shape[0] // n

    def wo_copy(s, c):
        part = pl.ds(pl.multiple_of(s * wo_piece, wo_piece), wo_piece)
        return remote(wo.at[part, :], wo_v.at[c, part, :], wo_s.at[s], wo_r.at[s], other)

    local = [pltpu.make_async_copy(wq, wq_v, loc.at[0])]
    if shared:
        local += [
            pltpu.make_async_copy(wk, raw.at[core, 0], loc.at[1]),
            pltpu.make_async_copy(wv, raw.at[core, 1], loc.at[2]),
        ]
    else:
        local += [
            pltpu.make_async_copy(wk, wkv_v.at[:, 0:HEAD_DIM], loc.at[1]),
            pltpu.make_async_copy(wv, wkv_v.at[:, HEAD_DIM:], loc.at[2]),
        ]
    own_wo = pltpu.make_async_copy(wo, wo_v.at[core], loc.at[3])

    barrier = pltpu.get_barrier_semaphore()
    for to in (prv, other):
        pl.semaphore_signal(barrier, inc=1, device_id=to, device_id_type=MESH)

    x = tokens[...].astype(F32)
    scale = lax.rsqrt(jnp.mean(x * x, axis=-1, keepdims=True) + 1e-05)
    normed[pl.ds(block_row(pos, core), rows), :] = (x * scale * gain[...]).astype(BF16)

    pl.semaphore_wait(barrier, 2)
    for h in range(HALVES):
        ring(0, h).start()
    for h in range(HALVES):
        fwd(0, h).start()
    if shared:
        kv = [
            remote(wk, raw.at[core, 0], kv_s.at[0], kv_r.at[0], other),
            remote(wv, raw.at[core, 1], kv_s.at[1], kv_r.at[1], other),
        ]
        for c in kv:
            c.start()
    for c in local:
        c.start()
    own_wo.start()

    def tables():
        drow = docs[...].astype(F32)
        doc_v[...] = jnp.transpose(jnp.broadcast_to(drow, (HEAD_DIM, count)))
        lane = lax.broadcasted_iota(jnp.int32, (1, HEAD_DIM), 1)
        sign = jnp.where(lane < HEAD_DIM // 2, F32(-1.0), F32(1.0))
        tile = 128

        def one(i, carry):
            at = pl.ds(pl.multiple_of(i * tile, tile), tile)
            less = (drow < doc_v[at, 0:1]).astype(F32)
            first = jnp.sum(less, axis=1, keepdims=True)
            index = (lax.broadcasted_iota(jnp.int32, (tile, 1), 0) + i * tile).astype(F32)
            angle = (index - first) * freq[...]
            cos_v[at, :] = jnp.cos(angle)
            sin_v[at, :] = jnp.sin(angle) * sign
            return carry

        lax.fori_loop(0, count // tile, one, 0)

    def join():
        if not shared:
            return
        for i in range(2):
            remote(wk, raw.at[1 - core, i], kv_s.at[i], kv_r.at[i], other).wait_recv()
        tall = 512

        def one(i, carry):
            at = pl.ds(pl.multiple_of(i * tall, tall), tall)
            wkv_v[at, :] = jnp.concatenate(
                [raw[0, 0, at, :], raw[1, 0, at, :], raw[0, 1, at, :], raw[1, 1, at, :]], axis=1
            )
            return carry

        lax.fori_loop(0, width // tall, one, 0)

    def rope(u, at):
        return u * cos_v[at, :] + pltpu.roll(u, HEAD_DIM // 2, 1) * sin_v[at, :]

    deep = 1024

    def product(starts, weights):
        def one(i, acc):
            k = pl.ds(pl.multiple_of(i * deep, deep), deep)
            left = jnp.concatenate([normed[pl.ds(a, rows), k] for a in starts], axis=0)
            return acc + jnp.dot(left, weights[k, :], preferred_element_type=F32)

        start = jnp.zeros((rows * len(starts), weights.shape[1]), F32)
        return lax.fori_loop(0, width // deep, one, start)

    def do_queries(starts):
        raw_q = product(starts, wq_v)
        for i, a in enumerate(starts):
            at = pl.ds(a, rows)
            for h in range(heads):
                u = raw_q[i * rows : (i + 1) * rows, h * HEAD_DIM : (h + 1) * HEAD_DIM]
                q_v[at, h * HEAD_DIM : (h + 1) * HEAD_DIM] = rope(u, at).astype(BF16)

    def do_keys(starts):
        both = product(starts, wkv_v)
        for i, a in enumerate(starts):
            at = pl.ds(a, rows)
            u = both[i * rows : (i + 1) * rows, :].astype(BF16)
            k_v[at, :] = rope(u[:, :HEAD_DIM].astype(F32), at).astype(BF16)
            v_v[at, :] = u[:, HEAD_DIM:]

    def group(s):
        return [block_row(pos - way * s, core), block_row(pos + way * s, 1 - core)]

    def step(s, carry):
        wo_copy(s, core).start()
        for h in range(HALVES):
            ring_in(s, h).wait_recv()

            @pl.when(s < n - 2)
            def _():
                ring(s + 1, h).start()

            fwd(s + 1, h).start()
            if h == 0:

                @pl.when(s == 0)
                def _():
                    for c in local:
                        c.wait()
                    join()

                @pl.when(s > 0)
                def _():
                    for k in range(HALVES):
                        fwd_in(s - 1, k).wait_recv()
                    do_queries(group(s - 1))

            if h == HALVES - 1:

                @pl.when(s == 0)
                def _():
                    tables()

                @pl.when(s > 0)
                def _():
                    do_keys(group(s - 1))

        return carry

    lax.fori_loop(0, n - 1, step, 0)
    wo_copy(n - 1, core).start()
    for s in (n - 2, n - 1):
        for h in range(HALVES):
            fwd_in(s, h).wait_recv()
    last = group(n - 2) + group(n - 1)
    do_keys(last)
    do_queries(last)

    def sent(s, carry):
        for h in range(HALVES):
            fwd(s, h).wait_send()

            @pl.when(s < n - 1)
            def _():
                ring(s, h).wait_send()

        wo_copy(s, core).wait_send()
        return carry

    lax.fori_loop(0, n, sent, 0)
    if shared:
        for c in kv:
            c.wait_send()

    block = 128
    root = F32(1.0 / HEAD_DIM**0.5)
    for i in range(count // block):
        seen = (i + 1) * block
        span = slice(i * block, seen)
        r_idx = lax.broadcasted_iota(jnp.int32, (block, seen), 0) + i * block
        c_idx = lax.broadcasted_iota(jnp.int32, (block, seen), 1)
        visible = (c_idx <= r_idx) & (docs[:, :seen].astype(F32) == doc_v[span, 0:1])
        for h in range(heads):
            hs = slice(h * HEAD_DIM, (h + 1) * HEAD_DIM)
            scores = lax.dot_general(
                q_v[span, hs], k_v[0:seen, :], (((1,), (1,)), ((), ())),
                preferred_element_type=F32,
            )
            scores = jnp.where(visible, scores * root, F32(-1e30))
            weights = jnp.exp(scores - jnp.max(scores, axis=-1, keepdims=True))
            total = jnp.sum(weights, axis=-1, keepdims=True)
            probs = (weights * (1.0 / total)).astype(BF16)
            result = jnp.dot(probs, v_v[0:seen, :], preferred_element_type=F32).astype(BF16)
            for j in range(block // rows):
                t = i * (block // rows) + j
                att_v[t % 2, (t // 2) * rows : (t // 2 + 1) * rows, hs] = result[
                    j * rows : (j + 1) * rows
                ]

    swap = remote(att_v.at[1 - core], att_in, at_s.at[0], at_r.at[0], other)
    swap.start()
    own_wo.wait()

    def arrived(s, carry):
        wo_copy(s, 1 - core).wait_recv()
        return carry

    lax.fori_loop(0, n, arrived, 0)
    swap.wait()

    def part_row(p):
        return pl.multiple_of(chip_of(n, at_pos(p)) * rows, rows)

    def part_of(p, k):
        return (pl.ds(part_row(p), rows), slice(k * cols, (k + 1) * cols))

    def reduced(s, k, src):
        dst = inbox.at[s, :, k * cols : (k + 1) * cols]
        return remote(src, dst, rs_s.at[s, k], rs_r.at[s, k], nxt)

    def first_out(k):
        at, cs = part_of(pos - way, k)
        return reduced(0, k, normed.at[at, cs])

    def later_out(s, k):
        return reduced(s, k, inbox.at[s - 1, :, k * cols : (k + 1) * cols])

    thin = 256
    for k in range(PARTS):

        def one(i, carry):
            cs = pl.ds(pl.multiple_of(k * cols + i * thin, thin), thin)
            out = jnp.dot(att_v[core], wo_v[core, :, cs], preferred_element_type=F32)
            out += jnp.dot(att_in[...], wo_v[1 - core, :, cs], preferred_element_type=F32)
            normed[0 : n * rows, cs] = out.astype(BF16)
            return carry

        lax.fori_loop(0, cols // thin, one, 0)
        first_out(k).start()

    def hop(s, carry):
        for k in range(PARTS):
            cs = slice(k * cols, (k + 1) * cols)
            reduced(s - 1, k, inbox.at[s - 1, :, cs]).wait_recv()
            at, _ = part_of(pos - way * (s + 1), k)
            both = inbox[s - 1, :, cs].astype(F32) + normed[at, cs].astype(F32)
            inbox[s - 1, :, cs] = both.astype(BF16)
            later_out(s, k).start()
        return carry

    lax.fori_loop(1, n - 1, hop, 0)
    for k in range(PARTS):
        cs = slice(k * cols, (k + 1) * cols)
        reduced(n - 2, k, inbox.at[n - 2, :, cs]).wait_recv()
        at, _ = part_of(pos, k)
        total = inbox[n - 2, :, cs].astype(F32) + normed[at, cs].astype(F32)
        att_out[:, cs] = total.astype(BF16)
        hid_out[:, cs] = (tokens[:, cs].astype(F32) + total).astype(BF16)

    for k in range(PARTS):
        first_out(k).wait_send()

    def left(s, carry):
        for k in range(PARTS):
            later_out(s, k).wait_send()
        return carry

    lax.fori_loop(1, n - 1, left, 0)


def body(tokens, attn_gain, w_query, w_key, w_value, w_output, doc_ids):
    n = lax.axis_size("tensor") // 2
    rows, width = tokens.shape
    count = doc_ids.shape[0]
    mine = w_query.shape[1]
    heads = mine // HEAD_DIM
    levels = (HEAD_DIM // w_key.shape[1]).bit_length() - 1
    shared = levels == 1
    if not shared:
        place = lax.axis_index("tensor")
        stacked = jnp.stack([w_key, w_value])
        for bit in range(levels):
            stacked = join_cols(stacked, swapped(stacked, "tensor", bit), place, bit)
        w_key, w_value = stacked[0], stacked[1]
    freq = F32(500000.0) ** (
        -(jnp.arange(HEAD_DIM // 2, dtype=F32) * 2.0 / HEAD_DIM)
    )
    freq = jnp.concatenate([freq, freq])[None, :]
    vmem = pl.BlockSpec(memory_space=pltpu.VMEM)
    hbm = pl.BlockSpec(memory_space=pl.ANY)
    raw = (2, 2, width, w_key.shape[1]) if shared else (2, 2, 16, HEAD_DIM)
    dma = pltpu.SemaphoreType.DMA
    return pl.pallas_call(
        functools.partial(kernel, n, heads, shared),
        out_shape=(jax.ShapeDtypeStruct((rows, width), BF16),) * 2,
        in_specs=[vmem, vmem, hbm, hbm, hbm, hbm, vmem, vmem],
        out_specs=(vmem, vmem),
        scratch_shapes=[
            pltpu.VMEM((count, width), BF16),
            pltpu.VMEM((width, mine), BF16),
            pltpu.VMEM(raw, BF16),
            pltpu.VMEM((width, 2 * HEAD_DIM), BF16),
            pltpu.VMEM((2, mine, width), BF16),
            pltpu.VMEM((count, mine), BF16),
            pltpu.VMEM((count, HEAD_DIM), BF16),
            pltpu.VMEM((count, HEAD_DIM), BF16),
            pltpu.VMEM((2, n * rows, mine), BF16),
            pltpu.VMEM((n * rows, mine), BF16),
            pltpu.VMEM((count, HEAD_DIM), F32),
            pltpu.VMEM((count, HEAD_DIM), F32),
            pltpu.VMEM((count, HEAD_DIM), F32),
            pltpu.VMEM((n - 1, rows, width), BF16),
            dma((n - 1, HALVES)), dma((n - 1, HALVES)),
            dma((n, HALVES)), dma((n, HALVES)),
            dma((2,)), dma((2,)),
            dma((n,)), dma((n,)),
            dma((1,)), dma((1,)),
            dma((n - 1, PARTS)), dma((n - 1, PARTS)),
            dma((4,)),
        ],
        compiler_params=pltpu.CompilerParams(
            collective_id=0, has_side_effects=True, vmem_limit_bytes=60 * 1024 * 1024
        ),
    )(tokens, attn_gain[None, :], w_query, w_key, w_value, w_output, doc_ids[None, :], freq)


def solution(mesh):
    placed = (
        P(("groups", "tensor"), None),
        P(),
        P(None, "tensor"),
        P(None, "tensor"),
        P(None, "tensor"),
        P("tensor", None),
        P("groups"),
    )
    return jax.shard_map(
        body,
        mesh=mesh,
        in_specs=placed,
        out_specs=(P(("groups", "tensor"), None), P(("groups", "tensor"), None)),
        check_vma=False,
    )
```

time: 232 us -> 122 us (0.53)
  waiting for transfers between devices: 172 us -> 0 us
  Pallas kernels: 0 us -> 111 us
  matrix products: 24.6 us -> 0 us
  other arithmetic: 16.7 us -> 0.6 us
  between operations: 14.2 us -> 0.64 us
  local copies, waits for them, and re-layouts: 3.21 us -> 9.23 us
    pallas_call x0 -> x1, Pallas kernels: none -> 111 us  [body(): pl.pallas_call(functools.partial(kernel, n, heads, shared), out_shape=(ja...]
    reduce_scatter x1 -> x0, waiting for transfers between devices: 103 us -> none  [body(): lax.psum_scatter(jnp.dot(attended, w_output, preferred_element_type=jnp.f...]
    all_gather x1 -> x0, waiting for transfers between devices: 66.1 us -> none  [body(): normed = lax.all_gather(normed_local, 'tensor', axis=0, tiled=True)]
    dot_general x5 -> x0, matrix products: 24.6 us -> none  [the longest x1 9.46 us: body(): jnp.dot(normed, w_query, preferred_element_type=jnp.float32)]
    unnamed x18 -> x4, local copies, waits for them, and re-layouts: 3.11 us -> 9.23 us
    convert_element_type x4 -> x0, other arithmetic: 4.02 us -> none  [the longest x1 2.03 us: body(): normed_local = (rows * lax.rsqrt(jnp.mean(rows * rows, axis=-1, keepdims=...]
    select_n x1 -> x0, other arithmetic: 3.92 us -> none  [join_cols(): lower_part = jnp.where(upper, other, mine)]
    another operation x3 -> x0, other arithmetic: 3.9 us -> none  [the longest x1 3.06 us: body(): stacked = jnp.stack([w_key, w_value])]
  transfers between devices with their start and end apart: 3 -> 0, of which waited for: 3 -> 0; matrix products, arithmetic and copies ran while one was open for 4% -> 0% of each run, Pallas kernels for 0% -> 0%
where the time goes in v1:
time: 122 us
  Pallas kernels  111 us (91%)
  local copies, waits for them, and re-layouts  9.23 us (8%)
    pallas_call x1, Pallas kernels, body(): pl.pallas_call(functools.partial(kernel, n, heads, shared), out_shape=(ja...  111 us
    unnamed x4, local copies, waits for them, and re-layouts  9.23 us

profile of v1, /device:TPU:0, one launch (start us, length us, event | category | flops | bytes accessed | tf_op | source)
XLA Modules:
  0.0 121.6 jit_solution(3504662391344707904)
XLA Ops:
  0.6 0.6 maximum_bitcast_fusion.freq
  1.2 2.8 %copy.9.wk = bf16[8192,64]{1,0:T(8,128)(2,1)} copy(bf16[8192,64]{0,1:T(8,128)(2,1)} %param.10) | data formatting | bytes 2097152 | tf_op args[3]
  4.0 2.7 %copy.10.wv = bf16[8192,64]{1,0:T(8,128)(2,1)} copy(bf16[8192,64]{0,1:T(8,128)(2,1)} %param.11) | data formatting | bytes 2097152 | tf_op args[4]
  6.7 111.1 %shard_map.86 = (bf16[32,8192]{1,0:T(8,128)(2,1)}, bf16[32,8192]{1,0:T(8,128)(2,1)}) custom-call(bf16[32,8192]{1,0:T(8,128)(2,1)} %tokens.1, f32[1,8192]{1,0:T(1,128)} %bitcast.4, bf16[8192,512]{1,0:T(8,128)(2,1)} %wq.1, bf16[8192,64]{1,0:T(8,128)(2,1)} %copy.9.wk, bf16[8192,64]{1,0:T(8,128)(2,1)} %copy.10.wv, bf16[512,8192]{1,0:T(8,128)(2,1)} %wo.1, ...), custom_call_target="tpu_custom_call" | custom-call | tf_op jit(solution)/shard_map/pallas_call | solution.py:387
  117.8 1.9 %copy.13 = bf16[32,8192]{1,0:T(8,128)(2,1)} copy(bf16[32,8192]{1,0:T(8,128)(2,1)} %get-tuple-element.4) | data formatting | bytes 1048576
  119.7 1.9 %copy.14 = bf16[32,8192]{1,0:T(8,128)(2,1)} copy(bf16[32,8192]{1,0:T(8,128)(2,1)} %get-tuple-element.5) | data formatting | bytes 1048576
  (1 shorter events, 0.0 us)

commit v2 on v1

--- a/solution.py
+++ b/solution.py
@@ -45,8 +45,8 @@
 def kernel(
     n, heads, shared,
     tokens, gain, wq, wk, wv, wo, docs, freq,
-    att_out, hid_out,
-    normed, wq_v, raw, wkv_v, wo_v, q_v, k_v, v_v, att_v, att_in, cos_v, sin_v, doc_v, inbox,
+    total_out,
+    normed, wq_v, wkv_v, wo_v, q_v, k_v, v_v, att_v, att_in, cos_v, sin_v, doc_v, inbox,
     ring_s, ring_r, fwd_s, fwd_r, kv_s, kv_r, wo_s, wo_r, at_s, at_r, rs_s, rs_r, loc,
 ):
     rows, width = tokens.shape
@@ -100,17 +100,17 @@
         part = pl.ds(pl.multiple_of(s * wo_piece, wo_piece), wo_piece)
         return remote(wo.at[part, :], wo_v.at[c, part, :], wo_s.at[s], wo_r.at[s], other)
 
-    local = [pltpu.make_async_copy(wq, wq_v, loc.at[0])]
-    if shared:
-        local += [
-            pltpu.make_async_copy(wk, raw.at[core, 0], loc.at[1]),
-            pltpu.make_async_copy(wv, raw.at[core, 1], loc.at[2]),
-        ]
-    else:
-        local += [
-            pltpu.make_async_copy(wk, wkv_v.at[:, 0:HEAD_DIM], loc.at[1]),
-            pltpu.make_async_copy(wv, wkv_v.at[:, HEAD_DIM:], loc.at[2]),
-        ]
+    kv_rows = wk.shape[0]
+
+    def kv_slot(c, i):
+        start = i * HEAD_DIM + (c * kv_rows if shared else 0)
+        return wkv_v.at[pl.ds(pl.multiple_of(start, 16), kv_rows), :]
+
+    local = [
+        pltpu.make_async_copy(wk, kv_slot(core, 0), loc.at[1]),
+        pltpu.make_async_copy(wv, kv_slot(core, 1), loc.at[2]),
+        pltpu.make_async_copy(wq, wq_v, loc.at[0]),
+    ]
     own_wo = pltpu.make_async_copy(wo, wo_v.at[core], loc.at[3])
 
     barrier = pltpu.get_barrier_semaphore()
@@ -128,8 +128,8 @@
         fwd(0, h).start()
     if shared:
         kv = [
-            remote(wk, raw.at[core, 0], kv_s.at[0], kv_r.at[0], other),
-            remote(wv, raw.at[core, 1], kv_s.at[1], kv_r.at[1], other),
+            remote(wk, kv_slot(core, 0), kv_s.at[0], kv_r.at[0], other),
+            remote(wv, kv_slot(core, 1), kv_s.at[1], kv_r.at[1], other),
         ]
         for c in kv:
             c.start()
@@ -156,38 +156,35 @@
 
         lax.fori_loop(0, count // tile, one, 0)
 
-    def join():
-        if not shared:
-            return
-        for i in range(2):
-            remote(wk, raw.at[1 - core, i], kv_s.at[i], kv_r.at[i], other).wait_recv()
-        tall = 512
-
-        def one(i, carry):
-            at = pl.ds(pl.multiple_of(i * tall, tall), tall)
-            wkv_v[at, :] = jnp.concatenate(
-                [raw[0, 0, at, :], raw[1, 0, at, :], raw[0, 1, at, :], raw[1, 1, at, :]], axis=1
-            )
-            return carry
-
-        lax.fori_loop(0, width // tall, one, 0)
+    def weights_in():
+        for c in local:
+            c.wait()
+        if shared:
+            for i in range(2):
+                remote(wk, kv_slot(1 - core, i), kv_s.at[i], kv_r.at[i], other).wait_recv()
 
     def rope(u, at):
         return u * cos_v[at, :] + pltpu.roll(u, HEAD_DIM // 2, 1) * sin_v[at, :]
 
     deep = 1024
 
-    def product(starts, weights):
+    def product(starts, weights, turned):
+        size = weights.shape[0] if turned else weights.shape[1]
+
         def one(i, acc):
             k = pl.ds(pl.multiple_of(i * deep, deep), deep)
             left = jnp.concatenate([normed[pl.ds(a, rows), k] for a in starts], axis=0)
+            if turned:
+                return acc + lax.dot_general(
+                    left, weights[:, k], (((1,), (1,)), ((), ())), preferred_element_type=F32
+                )
             return acc + jnp.dot(left, weights[k, :], preferred_element_type=F32)
 
-        start = jnp.zeros((rows * len(starts), weights.shape[1]), F32)
+        start = jnp.zeros((rows * len(starts), size), F32)
         return lax.fori_loop(0, width // deep, one, start)
 
     def do_queries(starts):
-        raw_q = product(starts, wq_v)
+        raw_q = product(starts, wq_v, False)
         for i, a in enumerate(starts):
             at = pl.ds(a, rows)
             for h in range(heads):
@@ -195,7 +192,7 @@
                 q_v[at, h * HEAD_DIM : (h + 1) * HEAD_DIM] = rope(u, at).astype(BF16)
 
     def do_keys(starts):
-        both = product(starts, wkv_v)
+        both = product(starts, wkv_v, True)
         for i, a in enumerate(starts):
             at = pl.ds(a, rows)
             u = both[i * rows : (i + 1) * rows, :].astype(BF16)
@@ -219,36 +216,40 @@
 
                 @pl.when(s == 0)
                 def _():
-                    for c in local:
-                        c.wait()
-                    join()
-
-                @pl.when(s > 0)
+                    tables()
+
+                @pl.when(s == 1)
+                def _():
+                    weights_in()
+                    for t in range(2):
+                        for k in range(HALVES):
+                            fwd_in(t, k).wait_recv()
+                    do_queries(group(0) + group(1))
+
+                @pl.when(s > 1)
                 def _():
                     for k in range(HALVES):
-                        fwd_in(s - 1, k).wait_recv()
-                    do_queries(group(s - 1))
+                        fwd_in(s, k).wait_recv()
+                    do_queries(group(s))
 
             if h == HALVES - 1:
 
-                @pl.when(s == 0)
+                @pl.when(s == 1)
                 def _():
-                    tables()
-
-                @pl.when(s > 0)
+                    do_keys(group(0) + group(1))
+
+                @pl.when(s > 1)
                 def _():
-                    do_keys(group(s - 1))
+                    do_keys(group(s))
 
         return carry
 
     lax.fori_loop(0, n - 1, step, 0)
     wo_copy(n - 1, core).start()
-    for s in (n - 2, n - 1):
-        for h in range(HALVES):
-            fwd_in(s, h).wait_recv()
-    last = group(n - 2) + group(n - 1)
-    do_keys(last)
-    do_queries(last)
+    for h in range(HALVES):
+        fwd_in(n - 1, h).wait_recv()
+    do_keys(group(n - 1))
+    do_queries(group(n - 1))
 
     def sent(s, carry):
         for h in range(HALVES):
@@ -268,7 +269,8 @@
 
     block = 128
     root = F32(1.0 / HEAD_DIM**0.5)
-    for i in range(count // block):
+    swaps = []
+    for i in reversed(range(count // block)):
         seen = (i + 1) * block
         span = slice(i * block, seen)
         r_idx = lax.broadcasted_iota(jnp.int32, (block, seen), 0) + i * block
@@ -291,8 +293,12 @@
                     j * rows : (j + 1) * rows
                 ]
 
-    swap = remote(att_v.at[1 - core], att_in, at_s.at[0], at_r.at[0], other)
-    swap.start()
+        part = pl.ds(i * block // 2, block // 2)
+        swap = remote(
+            att_v.at[1 - core, part, :], att_in.at[part, :], at_s.at[i], at_r.at[i], other
+        )
+        swap.start()
+        swaps.append(swap)
     own_wo.wait()
 
     def arrived(s, carry):
@@ -300,7 +306,8 @@
         return carry
 
     lax.fori_loop(0, n, arrived, 0)
-    swap.wait()
+    for swap in swaps:
+        swap.wait()
 
     def part_row(p):
         return pl.multiple_of(chip_of(n, at_pos(p)) * rows, rows)
@@ -348,8 +355,7 @@
         reduced(n - 2, k, inbox.at[n - 2, :, cs]).wait_recv()
         at, _ = part_of(pos, k)
         total = inbox[n - 2, :, cs].astype(F32) + normed[at, cs].astype(F32)
-        att_out[:, cs] = total.astype(BF16)
-        hid_out[:, cs] = (tokens[:, cs].astype(F32) + total).astype(BF16)
+        total_out[:, cs] = total
 
     for k in range(PARTS):
         first_out(k).wait_send()
@@ -382,18 +388,16 @@
     freq = jnp.concatenate([freq, freq])[None, :]
     vmem = pl.BlockSpec(memory_space=pltpu.VMEM)
     hbm = pl.BlockSpec(memory_space=pl.ANY)
-    raw = (2, 2, width, w_key.shape[1]) if shared else (2, 2, 16, HEAD_DIM)
     dma = pltpu.SemaphoreType.DMA
-    return pl.pallas_call(
+    total = pl.pallas_call(
         functools.partial(kernel, n, heads, shared),
-        out_shape=(jax.ShapeDtypeStruct((rows, width), BF16),) * 2,
+        out_shape=jax.ShapeDtypeStruct((rows, width), F32),
         in_specs=[vmem, vmem, hbm, hbm, hbm, hbm, vmem, vmem],
-        out_specs=(vmem, vmem),
+        out_specs=vmem,
         scratch_shapes=[
             pltpu.VMEM((count, width), BF16),
             pltpu.VMEM((width, mine), BF16),
-            pltpu.VMEM(raw, BF16),
-            pltpu.VMEM((width, 2 * HEAD_DIM), BF16),
+            pltpu.VMEM((2 * HEAD_DIM, width), BF16),
             pltpu.VMEM((2, mine, width), BF16),
             pltpu.VMEM((count, mine), BF16),
             pltpu.VMEM((count, HEAD_DIM), BF16),
@@ -408,14 +412,15 @@
             dma((n, HALVES)), dma((n, HALVES)),
             dma((2,)), dma((2,)),
             dma((n,)), dma((n,)),
-            dma((1,)), dma((1,)),
+            dma((count // 128,)), dma((count // 128,)),
             dma((n - 1, PARTS)), dma((n - 1, PARTS)),
             dma((4,)),
         ],
         compiler_params=pltpu.CompilerParams(
             collective_id=0, has_side_effects=True, vmem_limit_bytes=60 * 1024 * 1024
         ),
-    )(tokens, attn_gain[None, :], w_query, w_key, w_value, w_output, doc_ids[None, :], freq)
+    )(tokens, attn_gain[None, :], w_query, w_key.T, w_value.T, w_output, doc_ids[None, :], freq)
+    return (total.astype(BF16), (tokens.astype(F32) + total).astype(BF16))
 
 
 def solution(mesh):

time: 122 us -> 114 us (0.934)
  local copies, waits for them, and re-layouts: 9.23 us -> 0.01 us
  other arithmetic: 0.6 us -> 3.23 us
    unnamed x4 -> x2, local copies, waits for them, and re-layouts: 9.23 us -> 0.01 us
    convert_element_type x0 -> x1, other arithmetic: none -> 2.64 us  [body(): return (total.astype(BF16), (tokens.astype(F32) + total).astype(BF16))]
where the time goes in v2:
time: 114 us
  Pallas kernels  110 us (96%)
  other arithmetic  3.23 us (3%)
    pallas_call x1, Pallas kernels, body(): pl.pallas_call(functools.partial(kernel, n, heads, shared), out_shape=jax...  110 us
    convert_element_type x1, other arithmetic, body(): return (total.astype(BF16), (tokens.astype(F32) + total).astype(BF16))  2.64 us

profile of v2, /device:TPU:0, one launch (start us, length us, event | category | flops | bytes accessed | tf_op | source)
XLA Modules:
  0.0 114.2 jit_solution(1452400001468297416)
XLA Ops:
  0.6 0.6 maximum_bitcast_fusion.freq
  1.2 0.0 copy-start
  1.2 110.3 %shard_map.86 = f32[32,8192]{1,0:T(8,128)} custom-call(bf16[32,8192]{1,0:T(8,128)(2,1)} %tokens.1, f32[1,8192]{1,0:T(1,128)} %bitcast.8, bf16[8192,512]{1,0:T(8,128)(2,1)} %wq.1, bf16[64,8192]{1,0:T(8,128)(2,1)} %bitcast.6, bf16[64,8192]{1,0:T(8,128)(2,1)} %bitcast.7, bf16[512,8192]{1,0:T(8,128)(2,1)} %wo.1, s32[1,512]{1,0:T(1,128)} %bitcast.9, ...), custom_call_target="tpu_custom_call" | custom-call | tf_op jit(solution)/shard_map/pallas_call | solution.py:392
  111.5 0.0 copy-done
  111.6 2.6 %add_convert_fusion = (bf16[32,8192]{1,0:T(8,128)(2,1)}, bf16[32,8192]{1,0:T(8,128)(2,1)}) fusion(f32[32,8192]{1,0:T(8,128)} %shard_map.86, bf16[32,8192]{1,0:T(8,128)(2,1)S(1)} %copy-done), kind=kLoop, calls=%fused_computation | loop fusion | flops 1048576 | bytes 2621440 | tf_op jit(solution)/shard_map/convert_element_type | solution.py:423
  (1 shorter events, 0.0 us)
Async XLA Ops:
  1.2 110.3 %copy-start = (bf16[32,8192]{1,0:T(8,128)(2,1)S(1)}, bf16[32,8192]{1,0:T(8,128)(2,1)}, u32[]{:S(2)}) copy-start(bf16[32,8192]{1,0:T(8,128)(2,1)} %tokens.1) | copy-start | bytes 1572868

commit v3 on v2

--- a/solution.py
+++ b/solution.py
@@ -1,4 +1,5 @@
 import functools
+import math
 import jax
 import jax.numpy as jnp
 from jax import lax
@@ -8,7 +9,7 @@
 
 HEAD_DIM = 128
 HALVES = 2
-PARTS = 4
+PARTS = 8
 MESH = pl.DeviceIdType.MESH
 F32 = jnp.float32
 BF16 = jnp.bfloat16
@@ -44,7 +45,7 @@
 
 def kernel(
     n, heads, shared,
-    tokens, gain, wq, wk, wv, wo, docs, freq,
+    tokens, gain, wq, wk, wv, wo, docs,
     total_out,
     normed, wq_v, wkv_v, wo_v, q_v, k_v, v_v, att_v, att_in, cos_v, sin_v, doc_v, inbox,
     ring_s, ring_r, fwd_s, fwd_r, kv_s, kv_r, wo_s, wo_r, at_s, at_r, rs_s, rs_r, loc,
@@ -117,12 +118,13 @@
     for to in (prv, other):
         pl.semaphore_signal(barrier, inc=1, device_id=to, device_id_type=MESH)
 
-    x = tokens[...].astype(F32)
-    scale = lax.rsqrt(jnp.mean(x * x, axis=-1, keepdims=True) + 1e-05)
-    normed[pl.ds(block_row(pos, core), rows), :] = (x * scale * gain[...]).astype(BF16)
-
-    pl.semaphore_wait(barrier, 2)
     for h in range(HALVES):
+        x = tokens[h * piece : (h + 1) * piece, :].astype(F32)
+        scale = lax.rsqrt(jnp.mean(x * x, axis=-1, keepdims=True) + 1e-05)
+        at = pl.ds(pl.multiple_of(block_row(pos, core) + h * piece, piece), piece)
+        normed[at, :] = (x * scale * gain[...]).astype(BF16)
+        if h == 0:
+            pl.semaphore_wait(barrier, 2)
         ring(0, h).start()
     for h in range(HALVES):
         fwd(0, h).start()
@@ -142,6 +144,8 @@
         doc_v[...] = jnp.transpose(jnp.broadcast_to(drow, (HEAD_DIM, count)))
         lane = lax.broadcasted_iota(jnp.int32, (1, HEAD_DIM), 1)
         sign = jnp.where(lane < HEAD_DIM // 2, F32(-1.0), F32(1.0))
+        half = lax.rem(lane, HEAD_DIM // 2).astype(F32)
+        freq = jnp.exp(half * F32(-2.0 * math.log(500000.0) / HEAD_DIM))
         tile = 128
 
         def one(i, carry):
@@ -149,7 +153,7 @@
             less = (drow < doc_v[at, 0:1]).astype(F32)
             first = jnp.sum(less, axis=1, keepdims=True)
             index = (lax.broadcasted_iota(jnp.int32, (tile, 1), 0) + i * tile).astype(F32)
-            angle = (index - first) * freq[...]
+            angle = (index - first) * freq
             cos_v[at, :] = jnp.cos(angle)
             sin_v[at, :] = jnp.sin(angle) * sign
             return carry
@@ -166,7 +170,7 @@
     def rope(u, at):
         return u * cos_v[at, :] + pltpu.roll(u, HEAD_DIM // 2, 1) * sin_v[at, :]
 
-    deep = 1024
+    deep = 4096
 
     def product(starts, weights, turned):
         size = weights.shape[0] if turned else weights.shape[1]
@@ -276,23 +280,23 @@
         r_idx = lax.broadcasted_iota(jnp.int32, (block, seen), 0) + i * block
         c_idx = lax.broadcasted_iota(jnp.int32, (block, seen), 1)
         visible = (c_idx <= r_idx) & (docs[:, :seen].astype(F32) == doc_v[span, 0:1])
+        queries = jnp.concatenate(
+            [q_v[span, h * HEAD_DIM : (h + 1) * HEAD_DIM] for h in range(heads)], axis=0
+        )
+        scores = lax.dot_general(
+            queries, k_v[0:seen, :], (((1,), (1,)), ((), ())), preferred_element_type=F32
+        ).reshape(heads, block, seen)
+        scores = jnp.where(visible[None], scores * root, F32(-1e30))
+        weights = jnp.exp(scores - jnp.max(scores, axis=-1, keepdims=True))
+        total = jnp.sum(weights, axis=-1, keepdims=True)
+        probs = (weights * (1.0 / total)).astype(BF16).reshape(heads * block, seen)
+        result = jnp.dot(probs, v_v[0:seen, :], preferred_element_type=F32).astype(BF16)
         for h in range(heads):
-            hs = slice(h * HEAD_DIM, (h + 1) * HEAD_DIM)
-            scores = lax.dot_general(
-                q_v[span, hs], k_v[0:seen, :], (((1,), (1,)), ((), ())),
-                preferred_element_type=F32,
-            )
-            scores = jnp.where(visible, scores * root, F32(-1e30))
-            weights = jnp.exp(scores - jnp.max(scores, axis=-1, keepdims=True))
-            total = jnp.sum(weights, axis=-1, keepdims=True)
-            probs = (weights * (1.0 / total)).astype(BF16)
-            result = jnp.dot(probs, v_v[0:seen, :], preferred_element_type=F32).astype(BF16)
             for j in range(block // rows):
                 t = i * (block // rows) + j
-                att_v[t % 2, (t // 2) * rows : (t // 2 + 1) * rows, hs] = result[
-                    j * rows : (j + 1) * rows
+                att_v[t % 2, (t // 2) * rows : (t // 2 + 1) * rows, h * HEAD_DIM : (h + 1) * HEAD_DIM] = result[
+                    h * block + j * rows : h * block + (j + 1) * rows
                 ]
-
         part = pl.ds(i * block // 2, block // 2)
         swap = remote(
             att_v.at[1 - core, part, :], att_in.at[part, :], at_s.at[i], at_r.at[i], other
@@ -326,13 +330,14 @@
     def later_out(s, k):
         return reduced(s, k, inbox.at[s - 1, :, k * cols : (k + 1) * cols])
 
-    thin = 256
+    thin = 1024
     for k in range(PARTS):
 
         def one(i, carry):
             cs = pl.ds(pl.multiple_of(k * cols + i * thin, thin), thin)
-            out = jnp.dot(att_v[core], wo_v[core, :, cs], preferred_element_type=F32)
-            out += jnp.dot(att_in[...], wo_v[1 - core, :, cs], preferred_element_type=F32)
+            left = jnp.concatenate([att_v[core], att_in[...]], axis=1)
+            right = jnp.concatenate([wo_v[core, :, cs], wo_v[1 - core, :, cs]], axis=0)
+            out = jnp.dot(left, right, preferred_element_type=F32)
             normed[0 : n * rows, cs] = out.astype(BF16)
             return carry
 
@@ -382,17 +387,13 @@
         for bit in range(levels):
             stacked = join_cols(stacked, swapped(stacked, "tensor", bit), place, bit)
         w_key, w_value = stacked[0], stacked[1]
-    freq = F32(500000.0) ** (
-        -(jnp.arange(HEAD_DIM // 2, dtype=F32) * 2.0 / HEAD_DIM)
-    )
-    freq = jnp.concatenate([freq, freq])[None, :]
     vmem = pl.BlockSpec(memory_space=pltpu.VMEM)
     hbm = pl.BlockSpec(memory_space=pl.ANY)
     dma = pltpu.SemaphoreType.DMA
     total = pl.pallas_call(
         functools.partial(kernel, n, heads, shared),
         out_shape=jax.ShapeDtypeStruct((rows, width), F32),
-        in_specs=[vmem, vmem, hbm, hbm, hbm, hbm, vmem, vmem],
+        in_specs=[vmem, vmem, hbm, hbm, hbm, hbm, vmem],
         out_specs=vmem,
         scratch_shapes=[
             pltpu.VMEM((count, width), BF16),
@@ -419,7 +420,7 @@
         compiler_params=pltpu.CompilerParams(
             collective_id=0, has_side_effects=True, vmem_limit_bytes=60 * 1024 * 1024
         ),
-    )(tokens, attn_gain[None, :], w_query, w_key.T, w_value.T, w_output, doc_ids[None, :], freq)
+    )(tokens, attn_gain[None, :], w_query, w_key.T, w_value.T, w_output, doc_ids[None, :])
     return (total.astype(BF16), (tokens.astype(F32) + total).astype(BF16))
 
 

time: 114 us -> 105 us (0.921)
  Pallas kernels: 110 us -> 101 us
    pallas_call x1, Pallas kernels: 110 us -> 101 us  [body(): pl.pallas_call(functools.partial(kernel, n, heads, shared), out_shape=jax...]
where the time goes in v3:
time: 105 us
  Pallas kernels  101 us (96%)
  other arithmetic  2.64 us (3%)
    pallas_call x1, Pallas kernels, body(): pl.pallas_call(functools.partial(kernel, n, heads, shared), out_shape=jax...  101 us
    convert_element_type x1, other arithmetic, body(): return (total.astype(BF16), (tokens.astype(F32) + total).astype(BF16))  2.64 us

profile of v3, /device:TPU:0, one launch (start us, length us, event | category | flops | bytes accessed | tf_op | source)
XLA Modules:
  0.0 104.6 jit_solution(4861184840845831986)
XLA Ops:
  0.6 0.0 copy-start
  0.6 101.3 %shard_map.86 = f32[32,8192]{1,0:T(8,128)} custom-call(bf16[32,8192]{1,0:T(8,128)(2,1)} %tokens.1, f32[1,8192]{1,0:T(1,128)} %bitcast.6, bf16[8192,512]{1,0:T(8,128)(2,1)} %wq.1, bf16[64,8192]{1,0:T(8,128)(2,1)} %bitcast.4, bf16[64,8192]{1,0:T(8,128)(2,1)} %bitcast.5, bf16[512,8192]{1,0:T(8,128)(2,1)} %wo.1, s32[1,512]{1,0:T(1,128)} %bitcast.7), custom_call_target="tpu_custom_call" | custom-call | tf_op jit(solution)/shard_map/pallas_call | solution.py:393
  101.9 0.0 copy-done
  101.9 2.6 %add_convert_fusion = (bf16[32,8192]{1,0:T(8,128)(2,1)}, bf16[32,8192]{1,0:T(8,128)(2,1)}) fusion(f32[32,8192]{1,0:T(8,128)} %shard_map.86, bf16[32,8192]{1,0:T(8,128)(2,1)S(1)} %copy-done), kind=kLoop, calls=%fused_computation | loop fusion | flops 1048576 | bytes 2621440 | tf_op jit(solution)/shard_map/convert_element_type | solution.py:424
Async XLA Ops:
  0.6 101.3 %copy-start = (bf16[32,8192]{1,0:T(8,128)(2,1)S(1)}, bf16[32,8192]{1,0:T(8,128)(2,1)}, u32[]{:S(2)}) copy-start(bf16[32,8192]{1,0:T(8,128)(2,1)} %tokens.1) | copy-start | bytes 1572868

commit v4 on v3

--- a/solution.py
+++ b/solution.py
@@ -170,7 +170,7 @@
     def rope(u, at):
         return u * cos_v[at, :] + pltpu.roll(u, HEAD_DIM // 2, 1) * sin_v[at, :]
 
-    deep = 4096
+    deep = 8192
 
     def product(starts, weights, turned):
         size = weights.shape[0] if turned else weights.shape[1]
@@ -271,7 +271,7 @@
         for c in kv:
             c.wait_send()
 
-    block = 128
+    block = 256
     root = F32(1.0 / HEAD_DIM**0.5)
     swaps = []
     for i in reversed(range(count // block)):

time: 105 us -> 103 us (0.981)
    pallas_call x1, Pallas kernels: 101 us -> 100 us  [body(): pl.pallas_call(functools.partial(kernel, n, heads, shared), out_shape=jax...]
where the time goes in v4:
time: 103 us
  Pallas kernels  100 us (97%)
  other arithmetic  2.64 us (3%)
    pallas_call x1, Pallas kernels, body(): pl.pallas_call(functools.partial(kernel, n, heads, shared), out_shape=jax...  100 us
    convert_element_type x1, other arithmetic, body(): return (total.astype(BF16), (tokens.astype(F32) + total).astype(BF16))  2.64 us

profile of v4, /device:TPU:0, one launch (start us, length us, event | category | flops | bytes accessed | tf_op | source)
XLA Modules:
  0.0 103.3 jit_solution(5530516628389327196)
XLA Ops:
  0.6 0.0 copy-start
  0.6 100.0 %shard_map.86 = f32[32,8192]{1,0:T(8,128)} custom-call(bf16[32,8192]{1,0:T(8,128)(2,1)} %tokens.1, f32[1,8192]{1,0:T(1,128)} %bitcast.6, bf16[8192,512]{1,0:T(8,128)(2,1)} %wq.1, bf16[64,8192]{1,0:T(8,128)(2,1)} %bitcast.4, bf16[64,8192]{1,0:T(8,128)(2,1)} %bitcast.5, bf16[512,8192]{1,0:T(8,128)(2,1)} %wo.1, s32[1,512]{1,0:T(1,128)} %bitcast.7), custom_call_target="tpu_custom_call" | custom-call | tf_op jit(solution)/shard_map/pallas_call | solution.py:393
  100.7 0.0 copy-done
  100.7 2.6 %add_convert_fusion = (bf16[32,8192]{1,0:T(8,128)(2,1)}, bf16[32,8192]{1,0:T(8,128)(2,1)}) fusion(f32[32,8192]{1,0:T(8,128)} %shard_map.86, bf16[32,8192]{1,0:T(8,128)(2,1)S(1)} %copy-done), kind=kLoop, calls=%fused_computation | loop fusion | flops 1048576 | bytes 2621440 | tf_op jit(solution)/shard_map/convert_element_type | solution.py:424
Async XLA Ops:
  0.6 100.0 %copy-start = (bf16[32,8192]{1,0:T(8,128)(2,1)S(1)}, bf16[32,8192]{1,0:T(8,128)(2,1)}, u32[]{:S(2)}) copy-start(bf16[32,8192]{1,0:T(8,128)(2,1)} %tokens.1) | copy-start | bytes 1572868
